TPU v7x, 128 devices: a whole 4x4x4 slice. The times are simulated.
128 devices in a mesh: dp: 128 (over x, z, y, core).
Axes of the slice: x: 4, y: 4, z: 4, core: 2. Of those that a mesh axis runs over, the one named last changes fastest.
Arguments:
- queries: bfloat16 [16384, 768], P('dp'), may hold values from -2 to 2
- documents: bfloat16 [16384, 768], P('dp'), may hold values from -2 to 2
- positives: int32 [16384], P('dp'), may hold values from 0 to 16383, each once
Outputs:
- loss: float32 [], replicated
- grad_queries: float32 [16384, 768], P('dp')
- grad_documents: float32 [16384, 768], P('dp')
Inputs may be any that keep to these rules, and one draw needn't show every extreme that they name: `positives`: every document is the positive of exactly one query.
All inputs are finite; a program needn't handle non-finite values.
Results may differ from a plain program's by a relative error of at most 0.0004.
The roundings to bfloat16 on the way count: a program that leaves them out, or rounds other values in their place, can miss the bound.
Values may be sent and summed in bfloat16 or wider, within the bound.
No kernel may reach another device: no remote copies, remote signals or barrier semaphores. Data moves between devices by JAX's collectives and lax.ppermute only.
A program may use at most 192 MiB of HBM per device.

v0:
```python
import math

import jax
import jax.numpy as jnp
from jax import lax
from jax.sharding import PartitionSpec as P


def normalize(values):
    wide = values.astype(jnp.float32)
    length = jnp.sqrt(jnp.sum(wide * wide, axis=1, keepdims=True) + 1e-06)
    return (wide / length, length)


def contract_rows(left, right):
    return lax.dot_general(
        left, right, (((0,), (0,)), ((), ())), preferred_element_type=jnp.float32
    )


def contract_cols(left, right):
    return lax.dot_general(
        left, right, (((1,), (1,)), ((), ())), preferred_element_type=jnp.float32
    )


def local(queries, documents, positives):
    qn, qnorm = normalize(queries)
    dn, dnorm = normalize(documents)
    qb = qn.astype(jnp.bfloat16)
    db = dn.astype(jnp.bfloat16)
    count_q, width = qb.shape
    alldocs = lax.all_gather(db, "dp", axis=0, tiled=True)
    count_docs = alldocs.shape[0]
    block = math.gcd(count_docs, 1024)
    nblocks = count_docs // block
    blocks = alldocs.reshape(nblocks, block, width)
    starts = lax.iota(jnp.int32, nblocks) * block

    def add_total(total, rows):
        scores = 20.0 * contract_cols(qb, rows)
        return (total + jnp.sum(jnp.exp(scores - 20.0), axis=1), None)

    total, unused = lax.scan(add_total, jnp.zeros((count_q,), jnp.float32), blocks)
    lse = 20.0 + jnp.log(total)
    picked = jnp.take(alldocs, positives, axis=0)
    positive_score = 20.0 * jnp.sum(qb.astype(jnp.float32) * picked.astype(jnp.float32), axis=1)
    loss_sum = lax.psum(jnp.sum(lse - positive_score), "dp")
    loss = loss_sum / (count_q * lax.axis_size("dp"))

    def weights_of(rows, start):
        scores = 20.0 * contract_cols(qb, rows)
        columns = start + lax.iota(jnp.int32, rows.shape[0])
        hit = (positives[:, None] == columns[None, :]).astype(jnp.float32)
        return (jnp.exp(scores - lse[:, None]) - hit).astype(jnp.bfloat16)

    def add_grad(acc, item):
        rows, start = item
        weights = weights_of(rows, start)
        acc = acc + 20.0 * jnp.dot(weights, rows, preferred_element_type=jnp.float32)
        return (acc, None)

    gq, stacked = lax.scan(add_grad, jnp.zeros((count_q, width), jnp.float32), (blocks, starts))
    grad_queries = (gq - jnp.sum(gq * qn, axis=1, keepdims=True) * qn) / qnorm
    rows = alldocs
    gd = lax.psum_scatter(
        20.0 * contract_rows(weights_of(rows, jnp.int32(0)), qb),
        "dp",
        scatter_dimension=0,
        tiled=True,
    )
    grad_documents = (gd - jnp.sum(gd * dn, axis=1, keepdims=True) * dn) / dnorm
    return (loss, grad_queries, grad_documents)


def solution(mesh):
    placed = (P("dp", None), P("dp", None), P("dp"))
    return jax.shard_map(
        local,
        mesh=mesh,
        in_specs=placed,
        out_specs=(P(), P("dp", None), P("dp", None)),
        check_vma=False,
    )
```

profile of v0, /device:TPU:1, one launch (start us, length us, event | category | flops | bytes accessed | tf_op | source)
XLA Modules:
  0.0 501.5 jit_solution(16684824375589639476)
XLA Ops:
  12.5 96.0 %all-gather.2.cloned.1.call-done = bf16[16384,768]{1,0:T(8,128)(2,1)} async-done(((bf16[128,768]{1,0:T(8,128)(2,1)}), bf16[16384,768]{1,0:T(8,128)(2,1)}) %all-gather.2.cloned.1.call-update) | async-done | bytes 25165840 | tf_op jit(solution)/shard_map/all_gather | solution.py:33
  108.4 12.4 %gather_fusion = bf16[128,768]{1,0:T(8,128)(2,1)S(1)} fusion(bf16[16384,768]{1,0:T(8,128)(2,1)} %all-gather.2.cloned.1.call-done, s32[1024]{0:T(1024)S(1)} %pad_clamp_fusion), kind=kCustom, calls=%fused_computation | custom fusion | bytes 393728 | tf_op jit(solution)/shard_map/jit(_take)/gather | solution.py:46
  122.0 32.5 %while.24 = (s32[]{:T(128)}, f32[128]{0:T(128)S(1)}, bf16[16,1024,768]{2,1,0:T(8,128)(2,1)}, bf16[128,768]{1,0:T(8,128)(2,1)S(1)}, s32[]{:T(128)}, /*index=5*/s32[]{:T(128)}) while((s32[]{:T(128)}, f32[128]{0:T(128)S(1)}, bf16[16,1024,768]{2,1,0:T(8,128)(2,1)}, bf16[128,768]{1,0:T(8,128)(2,1)S(1)}, s32[]{:T(128)}, ...), condition=%wide.region_4.5_spmd.clone, body=%wide.region_2.4_spmd.clone.sunk | while | flops 201719936 | bytes 1771611 | solution.py:44
  126.0 2.0 fusion.86
  132.1 2.0 fusion.86
  134.2 2.0 fusion.86
  136.2 2.0 fusion.86
  138.2 2.0 fusion.86
  142.3 2.0 fusion.86
  144.3 2.0 fusion.86
  146.4 2.0 fusion.86
  152.5 2.0 fusion.86
  155.1 28.4 %convolution_multiply_fusion = f32[16384,768]{1,0:T(8,128)} fusion(bf16[128,768]{1,0:T(8,128)(2,1)S(1)} %get-tuple-element.279, bf16[16384,768]{1,0:T(8,128)(2,1)} %bitcast.64, s32[128]{0:T(128)S(1)} %copy-done.2, f32[128]{0:T(128)S(1)} %get-tuple-element.250), kind=kOutput, calls=%fused_computation.34 | convolution fusion | flops 6467616768 | bytes 75695104 | tf_op jit(solution)/shard_map/dot_general | solution.py:16
  183.6 64.5 %psum.7 = f32[]{:T(128)} all-reduce(f32[]{:T(128)} %get-tuple-element.159), channel_id=1, replica_groups=mesh['dp'=128] {'dp'}, use_global_device_ids=true, to_apply=%region_7.8 | all-reduce | flops 1 | bytes 8 | tf_op jit(solution)/shard_map/psum | solution.py:48
  248.8 72.9 %while.25 = (s32[]{:T(128)}, f32[128,768]{1,0:T(8,128)S(1)}, bf16[16,1024,768]{2,1,0:T(8,128)(2,1)}, bf16[128,768]{1,0:T(8,128)(2,1)S(1)}, f32[128]{0:T(128)S(1)...) while((s32[]{:T(128)}, f32[128,768]{1,0:T(8,128)S(1)}, ...), condition=%wide.region_9.10_spmd.clone, body=%wide.region_8.9_spmd.clone.sunk | while | flops 403735552 | bytes 4139646 | solution.py:63
  250.1 3.3 fusion.91
  254.6 3.3 fusion.91
  259.2 3.3 fusion.91
  263.7 3.3 fusion.91
  268.3 3.3 fusion.91
  272.9 3.3 fusion.91
  277.4 3.3 fusion.91
  282.0 3.3 fusion.91
  286.6 3.3 fusion.91
  291.2 3.3 fusion.91
  295.7 3.3 fusion.91
  300.2 3.3 fusion.91
  304.8 3.3 fusion.91
  309.3 3.3 fusion.91
  313.9 3.3 fusion.91
  318.4 3.3 fusion.91
  322.9 167.6 %reduce-scatter.2.cloned.1.call-done = f32[128,768]{1,0:T(8,128)} async-done(((f32[16384,768]{1,0:T(8,128)}), f32[128,768]{1,0:T(8,128)}) %reduce-scatter.2.cloned.1.call-update) | async-done | bytes 393232 | tf_op jit(solution)/shard_map/reduce_scatter | solution.py:66
  (82 shorter events, 45.2 us)
Async XLA Ops:
  7.2 147.9 %copy-start.2 = (s32[128]{0:T(128)S(1)}, s32[128]{0:T(128)}, u32[]{:S(2)}) copy-start(s32[128]{0:T(128)} %param.9) | copy-start | bytes 1540
  7.2 101.3 %all-gather.2.cloned.1.call-start = ((), (), s32[]{:S(2)}) async-start(), calls=%async_computation.1 | async-start | bytes 25362432 | tf_op jit(solution)/shard_map/all_gather | solution.py:33
  10.0 480.4 %reduce-scatter.2.cloned.1.call-start = ((), (), s32[]{:S(2)}) async-start(), calls=%async_computation.2 | async-start | bytes 50724864 | tf_op jit(solution)/shard_map/reduce_scatter | solution.py:66
  248.8 73.0 %copy-start.1 = (bf16[128,768]{1,0:T(8,128)(2,1)S(1)}, bf16[128,768]{1,0:T(8,128)(2,1)}, u32[]{:S(2)}) copy-start(bf16[128,768]{1,0:T(8,128)(2,1)} %param.7) | copy-start | bytes 589828
  248.8 241.6 %copy-start = (bf16[128,768]{1,0:T(8,128)(2,1)S(1)}, bf16[128,768]{1,0:T(8,128)(2,1)}, u32[]{:S(2)}) copy-start(bf16[128,768]{1,0:T(8,128)(2,1)} %param.8) | copy-start | bytes 589828
Sparse Core Ops, SparseCore 0:
  11.7 96.6 all-gather.1
  183.7 306.7 reduce-scatter.1
where the time goes:
time: 504 us; the launch traced here: 502 us
  waiting for transfers between devices  264 us (52%)
  matrix products  113 us (22%)
  blocking collectives  64.5 us (13%)
  local copies, waits for them, and re-layouts  21.8 us (4%)
  other arithmetic  21.7 us (4%)
  between operations  15.9 us (3%)
    reduce_scatter x1, waiting for transfers between devices, local(): lax.psum_scatter(20.0 * contract_rows(weights_of(rows, jnp.int32(0)), qb)...  168 us
    all_gather x1, waiting for transfers between devices, local(): alldocs = lax.all_gather(db, 'dp', axis=0, tiled=True)  96 us
    psum x1, blocking collectives, local(): loss_sum = lax.psum(jnp.sum(lse - positive_score), 'dp')  64.5 us
    dot_general x16, matrix products, add_grad(): jnp.dot(weights, rows, preferred_element_type=jnp.float32)  52.7 us
    dot_general x16, matrix products, contract_cols(): lax.dot_general(left, right, (((1,), (1,)), ((), ())), preferred_element_...  32 us
    dot_general x1, matrix products, contract_rows(): lax.dot_general(left, right, (((0,), (0,)), ((), ())), preferred_element_...  28.4 us
    gather x1, local copies, waits for them, and re-layouts, local(): picked = jnp.take(alldocs, positives, axis=0)  12.4 us
    add x16, other arithmetic, weights_of(): columns = start + lax.iota(jnp.int32, rows.shape[0])  10.4 us
  transfers between devices with their start and end apart: 2, of which 2 were waited for; matrix products, arithmetic and copies ran while one was open for 15% of the time, Pallas kernels for 0%

commit v1 on v0

v1 whole, which is shorter than its diff:
```python
import functools

import jax
import jax.numpy as jnp
from jax import lax
from jax.experimental import pallas as pl
from jax.experimental.pallas import tpu as pltpu
from jax.sharding import PartitionSpec as P

PAIRS_A = ((0, 1), (2, 3))
PAIRS_B = ((0, 3), (1, 2))
CUBE = 8
CORES = 2
PAD = 16
LOG2E = 1.4426950408889634


def device_index(x, z, y, core):
    return ((x * 4 + z) * 4 + y) * CORES + core


def cubes(pairs, core):
    return [
        [device_index(x, z, y, core) for x in px for z in pz for y in py]
        for px in pairs
        for pz in pairs
        for py in pairs
    ]


GROUPS_OWN = cubes(PAIRS_A, 0) + cubes(PAIRS_B, 1)
GROUPS_SUMS = cubes(PAIRS_A, 0) + cubes(PAIRS_A, 1)
SWAP = [(i, i ^ 1) for i in range(128)]


def normalize(values):
    wide = values.astype(jnp.float32)
    length = jnp.sqrt(jnp.sum(wide * wide, axis=1, keepdims=True) + 1e-06)
    return (wide / length, length)


def row_ids(block):
    rows = block.shape[0] - PAD
    tail = block[rows:, :rows].astype(jnp.float32)
    return tail[0:1, :] * 128.0 + tail[1:2, :]


def down_rows(row):
    return jnp.transpose(jnp.broadcast_to(row, (128, row.shape[1])))


def tile_kernel(role_ref, x_ref, y_ref, e_ref, stats_ref, cols_ref):
    step = pl.program_id(0)
    role = role_ref[0]
    block = e_ref.shape[0]
    x = x_ref[0, :block, :]

    @pl.when(step == 0)
    def _():
        cols_ref[...] = jnp.zeros_like(cols_ref)

    ids = down_rows(row_ids(x_ref[0]))
    partial = jnp.zeros((block, 128), jnp.float32)
    for k in range(CUBE):
        dots = lax.dot_general(
            x, y_ref[k, :block, :], (((1,), (1,)), ((), ())), preferred_element_type=jnp.float32
        )
        e = jnp.exp2(dots * (20.0 * LOG2E) - 20.0 * LOG2E)
        e_ref[:, k * block : (k + 1) * block] = e
        for h in range(block // 128):
            partial = partial + e[:, h * 128 : (h + 1) * 128]
        yids = row_ids(y_ref[k])
        columns = slice(k * block, (k + 1) * block)
        cols_ref[0:8, columns] += jnp.sum(e.reshape(block // 8, 8, block), axis=0)
        hit = jnp.where(jnp.concatenate([ids] * (block // 128), axis=1) == yids, dots, 0.0)
        cols_ref[8:16, columns] += jnp.sum(hit.reshape(block // 8, 8, block), axis=0)

    per = block // 128

    @pl.when(role == 0)
    def _():
        row = jnp.sum(jnp.transpose(partial), axis=0, keepdims=True)
        for h in range(per):
            piece = row[:, h * 128 : (h + 1) * 128]
            for g in range(CUBE):
                stats_ref[g, pl.ds(step * per + h, 1), :] = piece
                stats_ref[g, pl.ds(CUBE * per + step * per + h, 1), :] = jnp.zeros_like(piece)

    @pl.when((role == 1) & (step == CUBE - 1))
    def _():
        for part in range(2):
            col = jnp.sum(cols_ref[part * 8 : part * 8 + 8, :], axis=0, keepdims=True)
            for i in range(CUBE * per):
                for g in range(CUBE):
                    stats_ref[g, pl.ds(part * CUBE * per + i, 1), :] = col[:, i * 128 : (i + 1) * 128]


def grad_kernel(role_ref, e_ref, x_ref, y_ref, stats_ref, out_ref, y_all, scale_ref):
    step = pl.program_id(0)
    role = role_ref[0]
    block = e_ref.shape[0]
    per = block // 128
    half = CUBE * per

    @pl.when(step == 0)
    def _():
        for k in range(CUBE):
            y_all[k * block : (k + 1) * block, :] = y_ref[k, :block, :]
        total = jnp.sum(stats_ref[:, :half, :], axis=0)
        scale_ref[0:half, :] = 1.0 / total
        lse = 20.0 + jnp.log(total)
        picked = 20.0 * jnp.sum(stats_ref[:, half:, :], axis=0)
        scale_ref[half : half + 1, :] = jnp.broadcast_to(jnp.sum(lse - picked), (1, 128))

    ids = row_ids(x_ref[0])
    scale = [jnp.where(role == 0, scale_ref[pl.ds(step * per + h, 1), :], 1.0) for h in range(per)]
    scale = down_rows(jnp.concatenate(scale, axis=1))
    ids = down_rows(ids)
    ids = jnp.concatenate([ids] * per, axis=1)
    scale = jnp.concatenate([scale] * per, axis=1)
    weights = []
    for k in range(CUBE):
        col = [jnp.where(role == 1, scale_ref[k * per + h : k * per + h + 1, :], 1.0) for h in range(per)]
        col = jnp.concatenate(col, axis=1)
        hit = jnp.where(ids == row_ids(y_ref[k]), 1.0, 0.0)
        p = e_ref[:, k * block : (k + 1) * block] * scale * col
        weights.append((p - hit).astype(jnp.bfloat16))
    weights = jnp.concatenate(weights, axis=1)
    out_ref[0, :block, :] = 20.0 * jnp.dot(weights, y_all[...], preferred_element_type=jnp.float32)
    out_ref[0, block:, :] = jnp.broadcast_to(scale_ref[half : half + 1, 0:1], (8, out_ref.shape[2]))


def local(queries, documents, positives):
    me = lax.axis_index("dp")
    role = lax.rem(me, CORES)
    rows, width = queries.shape
    block = CORES * rows
    qn, qnorm = normalize(queries)
    dn, dnorm = normalize(documents)
    qb = qn.astype(jnp.bfloat16)
    db = dn.astype(jnp.bfloat16)
    first = role == 0

    def with_ids(values, ids):
        tail = jnp.stack([ids // 128, ids % 128]).astype(jnp.bfloat16)
        tail = jnp.pad(tail, ((0, PAD // 2 - 2), (0, width - rows)))
        return jnp.concatenate([values, tail], axis=0)

    mine = me * rows + lax.iota(jnp.int32, rows)
    qside = with_ids(qb, positives)
    dside = with_ids(db, mine)
    keep = jnp.where(first, qside, dside)
    come = lax.ppermute(jnp.where(first, dside, qside), "dp", SWAP)
    low = jnp.where(first, keep, come)
    high = jnp.where(first, come, keep)
    ids = jnp.concatenate([low[rows : rows + 2, :rows], high[rows : rows + 2, :rows]], axis=1)
    ids = jnp.pad(ids, ((0, PAD - 2), (0, width - block)))
    own = jnp.concatenate([low[:rows], high[:rows], ids], axis=0)
    sent = jnp.broadcast_to(own[None], (CUBE, block + PAD, width))
    x = lax.all_to_all(sent, "dp", 0, 0, axis_index_groups=GROUPS_OWN, tiled=True)
    y = lax.ppermute(x, "dp", SWAP)

    side = CUBE * block
    roles = role.reshape((1,)).astype(jnp.int32)
    per_block = pl.BlockSpec((1, block + PAD, width), lambda i: (i, 0, 0))
    whole = pl.BlockSpec((CUBE, block + PAD, width), lambda i: (0, 0, 0))
    tile_rows = pl.BlockSpec((block, side), lambda i: (i, 0))
    nstats = 2 * side // 128
    stats_spec = pl.BlockSpec((CUBE, nstats, 128), lambda i: (0, 0, 0))
    params = pltpu.CompilerParams(
        dimension_semantics=("arbitrary",), vmem_limit_bytes=56 * 1024 * 1024
    )
    e, stats = pl.pallas_call(
        tile_kernel,
        grid=(CUBE,),
        in_specs=[pl.BlockSpec(memory_space=pltpu.SMEM), per_block, whole],
        out_specs=[tile_rows, stats_spec],
        out_shape=[
            jax.ShapeDtypeStruct((side, side), jnp.float32),
            jax.ShapeDtypeStruct((CUBE, nstats, 128), jnp.float32),
        ],
        scratch_shapes=[pltpu.VMEM((16, side), jnp.float32)],
        compiler_params=params,
        name="tile",
    )(roles, x, y)
    stats = lax.all_to_all(stats, "dp", 0, 0, axis_index_groups=GROUPS_SUMS, tiled=True)
    parts = pl.pallas_call(
        grad_kernel,
        grid=(CUBE,),
        in_specs=[pl.BlockSpec(memory_space=pltpu.SMEM), tile_rows, per_block, whole, stats_spec],
        out_specs=pl.BlockSpec((1, block + 8, width), lambda i: (i, 0, 0)),
        out_shape=jax.ShapeDtypeStruct((CUBE, block + 8, width), jnp.float32),
        scratch_shapes=[
            pltpu.VMEM((side, width), jnp.bfloat16),
            pltpu.VMEM((side // 128 + 8, 128), jnp.float32),
        ],
        compiler_params=params,
        name="grad",
    )(roles, e, x, y, stats)
    parts = lax.all_to_all(parts, "dp", 0, 0, axis_index_groups=GROUPS_OWN, tiled=True)
    total = jnp.sum(parts, axis=0)
    low, high, tail = total[:rows], total[rows:block], total[block:]
    come = lax.ppermute(jnp.concatenate([jnp.where(first, high, low), tail], axis=0), "dp", SWAP)
    kept = jnp.where(first, low, high)
    gq = jnp.where(first, kept, come[:rows])
    gd = jnp.where(first, come[:rows], kept)
    loss = jnp.where(first, come[rows, 0], tail[0, 0]) / (rows * lax.axis_size("dp"))
    grad_queries = (gq - jnp.sum(gq * qn, axis=1, keepdims=True) * qn) / qnorm
    grad_documents = (gd - jnp.sum(gd * dn, axis=1, keepdims=True) * dn) / dnorm
    return (loss, grad_queries, grad_documents)


def solution(mesh):
    placed = (P("dp", None), P("dp", None), P("dp"))
    return jax.shard_map(
        local,
        mesh=mesh,
        in_specs=placed,
        out_specs=(P(), P("dp", None), P("dp", None)),
        check_vma=False,
    )
```

time: 504 us -> 148 us (0.29)
  waiting for transfers between devices: 264 us -> 8.26 us
  matrix products: 113 us -> 0 us
  Pallas kernels: 0 us -> 29.6 us
  blocking collectives: 64.5 us -> 92.1 us
  local copies, waits for them, and re-layouts: 21.8 us -> 3.04 us
  between operations: 15.9 us -> 3.21 us
  other arithmetic: 21.7 us -> 9.08 us
    reduce_scatter x1 -> x0, waiting for transfers between devices: 168 us -> none  [local(): lax.psum_scatter(20.0 * contract_rows(weights_of(rows, jnp.int32(0)), qb)...]
    dot_general x33 -> x0, matrix products: 113 us -> none  [the longest x16 52.7 us: add_grad(): jnp.dot(weights, rows, preferred_element_type=jnp.float32)]
    all_gather x1 -> x0, waiting for transfers between devices: 96 us -> none  [local(): alldocs = lax.all_gather(db, 'dp', axis=0, tiled=True)]
    all_to_all x0 -> x3, blocking collectives: none -> 92.1 us  [the longest x1 47.9 us: local(): lax.all_to_all(parts, 'dp', 0, 0, axis_index_groups=GROUPS_OWN, tiled=True)]
    psum x1 -> x0, blocking collectives: 64.5 us -> none  [local(): loss_sum = lax.psum(jnp.sum(lse - positive_score), 'dp')]
    pallas_call x0 -> x2, Pallas kernels: none -> 29.6 us  [the longest x1 16.1 us: local(): pl.pallas_call(grad_kernel, grid=(CUBE,), in_specs=[pl.BlockSpec(memory_s...]
    gather x1 -> x0, local copies, waits for them, and re-layouts: 12.4 us -> none  [local(): picked = jnp.take(alldocs, positives, axis=0)]
    add x33 -> x0, other arithmetic: 11.2 us -> none  [the longest x16 10.4 us: weights_of(): columns = start + lax.iota(jnp.int32, rows.shape[0])]
  transfers between devices with their start and end apart: 2 -> 3, of which waited for: 2 -> 3; matrix products, arithmetic and copies ran while one was open for 15% -> 0% of each run, Pallas kernels for 0% -> 0%
where the time goes in v1:
time: 148 us; the launch traced here: 147 us
  blocking collectives  92.1 us (62%)
  Pallas kernels  29.6 us (20%)
  other arithmetic  9.08 us (6%)
  waiting for transfers between devices  8.26 us (6%)
  between operations  3.21 us (2%)
  local copies, waits for them, and re-layouts  3.04 us (2%)
  starting transfers between devices  1.59 us (1%)
    all_to_all x1, blocking collectives, local(): lax.all_to_all(parts, 'dp', 0, 0, axis_index_groups=GROUPS_OWN, tiled=True)  47.9 us
    all_to_all x1, blocking collectives, local(): lax.all_to_all(sent, 'dp', 0, 0, axis_index_groups=GROUPS_OWN, tiled=True)  35.3 us
    pallas_call x1, Pallas kernels, local(): pl.pallas_call(grad_kernel, grid=(CUBE,), in_specs=[pl.BlockSpec(memory_s...  16.1 us
    pallas_call x1, Pallas kernels, local(): pl.pallas_call(tile_kernel, grid=(CUBE,), in_specs=[pl.BlockSpec(memory_s...  13.5 us
    all_to_all x1, blocking collectives, local(): lax.all_to_all(stats, 'dp', 0, 0, axis_index_groups=GROUPS_SUMS, tiled=True)  8.94 us
    ppermute x1, waiting for transfers between devices, local(): y = lax.ppermute(x, 'dp', SWAP)  5.94 us
    reduce_sum x1, other arithmetic, local(): total = jnp.sum(parts, axis=0)  3.4 us
  transfers between devices with their start and end apart: 3, of which 3 were waited for; matrix products, arithmetic and copies ran while one was open for 0% of the time, Pallas kernels for 0%

profile of v1, /device:TPU:1, one launch (start us, length us, event | category | flops | bytes accessed | tf_op | source)
XLA Modules:
  0.0 146.9 jit_solution(6080648792756804261)
XLA Ops:
  0.6 1.0 fusion
  1.7 1.1 fusion.1
  2.8 0.7 convert_bitcast_fusion
  3.5 1.2 fusion.23
  4.7 0.1 broadcast_select_fusion.2
  4.7 1.5 %collective-permute-start = (bf16[136,768]{1,0:T(8,128)(2,1)S(1)}, bf16[136,768]{1,0:T(8,128)(2,1)S(1)}, u32[]{:S(2)}, u32[]{:S(2)}) collective-permute-start(bf16[136,768]{1,0:T(8,128)(2,1)S(1)} %broadcast_select_fusion.2), channel_id=1, source_target_pairs={{0,1},{1,0},{2,3},{3,2},{4,5},{5,4},{6,7},{7,6},{8,9},{9,8},{10,11... | collective-permute-start | bytes 626696 | tf_op jit(solution)/shard_map/ppermute | solution.py:153
  6.2 1.1 collective-permute-done
  7.3 0.1 broadcast_select_fusion.1
  7.5 0.2 broadcast_in_dim.2
  7.8 35.3 %all_to_all.15.x_ref = bf16[8,272,768]{2,1,0:T(8,128)(2,1)S(1)} all-to-all(bf16[8,272,768]{2,1,0:T(8,128)(2,1)S(1)} %broadcast_in_dim.2), channel_id=1, replica_groups={{0,2,8,10,32,34,40,42},{4,6,12,14,36,38,44,46},{16,18,24,26,48,50,56,58..., dimensions={0} | all-to-all | bytes 6684672 | tf_op jit(solution)/shard_map/all_to_all | solution.py:160
  43.0 0.0 copy-start
  43.0 0.0 collective-permute-start.1
  43.0 5.9 %collective-permute-done.1.y_ref = bf16[8,272,768]{2,1,0:T(8,128)(2,1)S(1)} collective-permute-done((bf16[8,272,768]{2,1,0:T(8,128)(2,1)S(1)}, bf16[8,272,768]{2,1,0:T(8,128)(2,1)S(1)}, u32[]{:S(2)}, u32[]{:S(2)}) %collective-permute-start.1) | collective-permute-done | bytes 3342368 | tf_op jit(solution)/shard_map/ppermute | solution.py:161
  48.9 0.0 copy-start.1
  49.0 0.0 copy-done
  49.0 1.7 %copy-done.1 = bf16[8,272,768]{2,1,0:T(8,128)(2,1)} copy-done((bf16[8,272,768]{2,1,0:T(8,128)(2,1)}, bf16[8,272,768]{2,1,0:T(8,128)(2,1)S(1)}, u32[]{:S(2)}) %copy-start.1) | copy-done | bytes 3342360
  50.7 13.5 %tile.1 = (f32[2048,2048]{1,0:T(8,128)}, f32[8,32,128]{2,1,0:T(8,128)}) custom-call(s32[1]{0:T(128)} %bitcast.role_ref, bf16[8,272,768]{2,1,0:T(8,128)(2,1)} %copy-done, bf16[8,272,768]{2,1,0:T(8,128)(2,1)} %copy-done.1), custom_call_target="tpu_custom_call" | custom-call | tf_op jit(solution)/shard_map/tile/pallas_call | solution.py:173
  64.2 8.9 %all_to_all.16.stats_ref = f32[8,32,128]{2,1,0:T(8,128)} all-to-all(f32[8,32,128]{2,1,0:T(8,128)} %get-tuple-element.6), channel_id=1, replica_groups={{0,2,8,10,32,34,40,42},{4,6,12,14,36,38,44,46},{16,18,24,26,48,50,56,58..., dimensions={0} | all-to-all | bytes 262144 | tf_op jit(solution)/shard_map/all_to_all | solution.py:186
  73.1 16.1 %grad.1 = f32[8,264,768]{2,1,0:T(8,128)} custom-call(s32[1]{0:T(128)} %bitcast.role_ref, f32[2048,2048]{1,0:T(8,128)} %get-tuple-element.5.e_ref, bf16[8,272,768]{2,1,0:T(8,128)(2,1)} %copy-done, bf16[8,272,768]{2,1,0:T(8,128)(2,1)} %copy-done.1, f32[8,32,128]{2,1,0:T(8,128)} %all_to_all.16.stats_ref), custom_call_target="tpu_custom_call" | custom-call | tf_op jit(solution)/shard_map/grad/pallas_call | solution.py:187
  89.2 47.9 %all_to_all.17 = f32[8,264,768]{2,1,0:T(8,128)} all-to-all(f32[8,264,768]{2,1,0:T(8,128)} %grad.1), channel_id=1, replica_groups={{0,2,8,10,32,34,40,42},{4,6,12,14,36,38,44,46},{16,18,24,26,48,50,56,58..., dimensions={0} | all-to-all | bytes 12976128 | tf_op jit(solution)/shard_map/all_to_all | solution.py:200
  137.1 0.0 copy-start.2
  137.1 0.0 copy-start.3
  137.1 3.4 %reduce_sum.47 = f32[264,768]{1,0:T(8,128)S(1)} reduce(f32[8,264,768]{2,1,0:T(8,128)} %all_to_all.17, f32[]{:T(128)} %constant.49.clone.1), dimensions={0}, to_apply=%region_2.3 | reduce | flops 1419264 | bytes 7299076 | tf_op jit(solution)/shard_map/reduce_sum | solution.py:201
  140.6 0.1 collective-permute-start.2
  140.7 0.5 slice.50
  141.2 1.2 collective-permute-done.2
  142.5 0.5 slice.49
  144.3 0.0 copy-done.2
  144.3 0.0 copy-done.3
  144.3 0.3 multiply_reduce_fusion
  144.6 1.1 subtract_divide_fusion
  (14 shorter events, 0.2 us)
Async XLA Ops:
  4.7 2.6 %collective-permute-start = (bf16[136,768]{1,0:T(8,128)(2,1)S(1)}, bf16[136,768]{1,0:T(8,128)(2,1)S(1)}, u32[]{:S(2)}, u32[]{:S(2)}) collective-permute-start(bf16[136,768]{1,0:T(8,128)(2,1)S(1)} %broadcast_select_fusion.2), channel_id=1, source_target_pairs={{0,1},{1,0},{2,3},{3,2},{4,5},{5,4},{6,7},{7,6},{8,9},{9,8},{10,11... | collective-permute-start | bytes 626696 | tf_op jit(solution)/shard_map/ppermute | solution.py:153
  43.0 5.9 %copy-start = (bf16[8,272,768]{2,1,0:T(8,128)(2,1)}, bf16[8,272,768]{2,1,0:T(8,128)(2,1)S(1)}, u32[]{:S(2)}) copy-start(bf16[8,272,768]{2,1,0:T(8,128)(2,1)S(1)} %all_to_all.15.x_ref) | copy-start | bytes 10027012
  43.0 5.9 %collective-permute-start.1 = (bf16[8,272,768]{2,1,0:T(8,128)(2,1)S(1)}, bf16[8,272,768]{2,1,0:T(8,128)(2,1)S(1)}, u32[]{:S(2)}, u32[]{:S(2)}) collective-permute-start(bf16[8,272,768]{2,1,0:T(8,128)(2,1)S(1)} %all_to_all.15.x_ref), channel_id=1, source_target_pairs={{0,1},{1,0},{2,3},{3,2},{4,5},{5,4},{6,7},{7,6},{8,9},{9,8},{10,11... | collective-permute-start | bytes 10027016 | tf_op jit(solution)/shard_map/ppermute | solution.py:161
  48.9 1.8 %copy-start.1 = (bf16[8,272,768]{2,1,0:T(8,128)(2,1)}, bf16[8,272,768]{2,1,0:T(8,128)(2,1)S(1)}, u32[]{:S(2)}) copy-start(bf16[8,272,768]{2,1,0:T(8,128)(2,1)S(1)} %collective-permute-done.1.y_ref) | copy-start | bytes 10027012
  137.1 7.2 %copy-start.2 = (bf16[128,768]{1,0:T(8,128)(2,1)S(1)}, bf16[128,768]{1,0:T(8,128)(2,1)}, u32[]{:S(2)}) copy-start(bf16[128,768]{1,0:T(8,128)(2,1)} %param.3) | copy-start | bytes 589828
  137.1 7.2 %copy-start.3 = (bf16[128,768]{1,0:T(8,128)(2,1)S(1)}, bf16[128,768]{1,0:T(8,128)(2,1)}, u32[]{:S(2)}) copy-start(bf16[128,768]{1,0:T(8,128)(2,1)} %param.4) | copy-start | bytes 589828
  140.6 1.8 %collective-permute-start.2 = (f32[136,768]{1,0:T(8,128)S(1)}, f32[136,768]{1,0:T(8,128)S(1)}, u32[]{:S(2)}, u32[]{:S(2)}) collective-permute-start(f32[136,768]{1,0:T(8,128)S(1)} %pad_maximum_fusion.1), channel_id=1, source_target_pairs={{0,1},{1,0},{2,3},{3,2},{4,5},{5,4},{6,7},{7,6},{8,9},{9,8},{10,11... | collective-permute-start | bytes 1253384 | tf_op jit(solution)/shard_map/ppermute | solution.py:203

commit v2 on v0

v2 whole, which is shorter than its diff:
```python
import functools

import jax
import jax.numpy as jnp
from jax import lax
from jax.experimental import pallas as pl
from jax.experimental.pallas import tpu as pltpu
from jax.sharding import PartitionSpec as P

PAIRS_A = ((0, 1), (2, 3))
PAIRS_B = ((0, 3), (1, 2))
CUBE = 8
CORES = 2
ROWS = 128
BLOCK = CORES * ROWS
SIDE = CUBE * BLOCK
WIDTH = 768
PAD = 16
LOSS = 8
PER = BLOCK // 128
HALF = CUBE * PER
LOG2E = 1.4426950408889634
F32 = jnp.float32
BF16 = jnp.bfloat16


def device_index(x, z, y, core):
    return ((x * 4 + z) * 4 + y) * CORES + core


def partners(bits):
    moves = []
    for x in range(4):
        for z in range(4):
            for y in range(4):
                for core in range(CORES):
                    flip = (lambda v: v ^ 1) if core == 0 else (lambda v: 3 - v)
                    to = [flip(v) if bits & bit else v for v, bit in ((x, 4), (z, 2), (y, 1))]
                    moves.append((device_index(x, z, y, core), device_index(*to, core)))
    return moves


def a_cubes():
    return [
        [device_index(x, z, y, core) for x in px for z in pz for y in py]
        for core in range(CORES)
        for px in PAIRS_A
        for pz in PAIRS_A
        for py in PAIRS_A
    ]


SWAP = [(i, i ^ 1) for i in range(128)]
SUM_GROUPS = a_cubes()


def send(value, bits):
    return lax.ppermute(value, "dp", partners(bits))


def swap(value):
    return lax.ppermute(value, "dp", SWAP)


def near(value):
    return pltpu.with_memory_space_constraint(value, pltpu.VMEM)


def call(kernel, name, out_shape, *args, scratch=(), limit=8):
    return pl.pallas_call(
        kernel,
        name=name,
        out_shape=out_shape,
        scratch_shapes=scratch,
        compiler_params=pltpu.CompilerParams(vmem_limit_bytes=limit * 1024 * 1024),
    )(*args)


def role_of():
    return lax.axis_index("dp") & 1


def unit_rows(values):
    wide = values.astype(F32)
    length = jnp.sqrt(jnp.sum(wide * wide, axis=1, keepdims=True) + 1e-06)
    return wide / length, length


def row_ids(block_ref):
    tail = block_ref[BLOCK:, :BLOCK].astype(F32)
    return tail[0:1, :] * 128.0 + tail[1:2, :]


def down_rows(row, width):
    wide = jnp.transpose(jnp.broadcast_to(row, (128, row.shape[1])))
    return jnp.concatenate([wide] * (width // 128), axis=1)


def pre_kernel(q_ref, d_ref, p_ref, keep_ref, send_ref):
    me = lax.axis_index("dp")
    role = role_of()

    def fill(ref, values, ids):
        ref[:ROWS, :] = unit_rows(values)[0].astype(BF16)
        high = ids >> 7
        rows = lax.broadcasted_iota(jnp.int32, (PAD, ROWS), 0)
        tail = jnp.where(rows == 0, high, jnp.where(rows == 1, ids - high * 128, 0))
        ref[ROWS:, :] = jnp.zeros((PAD, WIDTH), BF16)
        ref[ROWS:, :ROWS] = tail.astype(F32).astype(BF16)

    mine = me * ROWS + lax.broadcasted_iota(jnp.int32, (1, ROWS), 1)

    @pl.when(role == 0)
    def _():
        fill(keep_ref, q_ref[...], p_ref[...])
        fill(send_ref, d_ref[...], mine)

    @pl.when(role == 1)
    def _():
        fill(keep_ref, d_ref[...], mine)
        fill(send_ref, q_ref[...], p_ref[...])


def join_kernel(keep_ref, come_ref, own_ref):
    def fill(low, high):
        own_ref[:ROWS, :] = low[:ROWS, :]
        own_ref[ROWS:BLOCK, :] = high[:ROWS, :]
        own_ref[BLOCK:, :] = jnp.zeros((PAD, WIDTH), BF16)
        own_ref[BLOCK:, :ROWS] = low[ROWS:, :ROWS]
        own_ref[BLOCK:, ROWS:BLOCK] = high[ROWS:, :ROWS]

    role = role_of()

    @pl.when(role == 0)
    def _():
        fill(keep_ref, come_ref)

    @pl.when(role == 1)
    def _():
        fill(come_ref, keep_ref)


def place_in_cube():
    me = lax.axis_index("dp")
    return ((me >> 5) & 1) * 4 + ((me >> 3) & 1) * 2 + ((me >> 1) & 1)


def tile_kernel(*refs):
    x, y, (e_ref, stats_ref, cols_ref) = refs[:CUBE], refs[CUBE : 2 * CUBE], refs[2 * CUBE :]
    place = place_in_cube()

    def block_of(i, k):
        dots = lax.dot_general(
            x[i][:BLOCK, :], y[k][:BLOCK, :], (((1,), (1,)), ((), ())), preferred_element_type=F32
        )
        e = jnp.exp2(dots * (20.0 * LOG2E) - 20.0 * LOG2E)
        e_ref[i * BLOCK : (i + 1) * BLOCK, k * BLOCK : (k + 1) * BLOCK] = e
        return dots, e

    def put(part, k, row):
        at = (place ^ k) * PER + part * HALF
        for h in range(PER):
            for g in range(CUBE):
                stats_ref[g, pl.ds(at + h, 1), :] = row[:, h * 128 : (h + 1) * 128]

    @pl.when(role_of() == 0)
    def _():
        for i in range(CUBE):
            partial = None
            for k in range(CUBE):
                _, e = block_of(i, k)
                for h in range(PER):
                    piece = e[:, h * 128 : (h + 1) * 128]
                    partial = piece if partial is None else partial + piece
            put(0, i, jnp.sum(jnp.transpose(partial), axis=0, keepdims=True))
            put(1, i, jnp.zeros((1, BLOCK), F32))

    @pl.when(role_of() == 1)
    def _():
        for i in range(CUBE):
            ids = down_rows(row_ids(x[i]), BLOCK)
            for k in range(CUBE):
                dots, e = block_of(i, k)
                hit = jnp.where(ids == row_ids(y[k]), dots, 0.0)
                columns = slice(k * BLOCK, (k + 1) * BLOCK)
                for part, value in enumerate((e, hit)):
                    value = jnp.sum(value.reshape(BLOCK // 8, 8, BLOCK), axis=0)
                    at = slice(part * 8, part * 8 + 8)
                    cols_ref[at, columns] = value if i == 0 else cols_ref[at, columns] + value
        for k in range(CUBE):
            for part in range(2):
                column = cols_ref[part * 8 : part * 8 + 8, k * BLOCK : (k + 1) * BLOCK]
                put(part, k, jnp.sum(column, axis=0, keepdims=True))


def grad_kernel(chosen, *refs):
    e_ref, stats_ref = refs[:2]
    y = refs[2 : 2 + CUBE]
    xs = refs[2 + CUBE : 2 + CUBE + len(chosen)]
    outs = refs[2 + CUBE + len(chosen) : -1]
    scale_ref = refs[-1]
    place = place_in_cube()
    total = jnp.sum(stats_ref[:, :HALF, :], axis=0)
    scale_ref[0:HALF, :] = 1.0 / total
    lse = 20.0 + jnp.log(total)
    picked = 20.0 * jnp.sum(stats_ref[:, HALF:, :], axis=0)
    loss = jnp.sum(lse - picked)

    def scale_of(k):
        at = (place ^ k) * PER
        return jnp.concatenate([scale_ref[pl.ds(at + h, 1), :] for h in range(PER)], axis=1)

    def body(role):
        for n, i in enumerate(chosen):
            ids = down_rows(row_ids(xs[n]), BLOCK)
            scale = down_rows(scale_of(i), BLOCK) if role == 0 else None
            acc = None
            for k in range(CUBE):
                if role == 1:
                    scale = scale_of(k)
                e = e_ref[i * BLOCK : (i + 1) * BLOCK, k * BLOCK : (k + 1) * BLOCK]
                weights = (e * scale - jnp.where(ids == row_ids(y[k]), 1.0, 0.0)).astype(BF16)
                part = jnp.dot(weights, y[k][:BLOCK, :], preferred_element_type=F32)
                acc = part if acc is None else acc + part
            outs[n][:BLOCK, :] = 20.0 * acc
            outs[n][BLOCK:, :] = jnp.full((LOSS, WIDTH), loss, F32)

    pl.when(role_of() == 0)(functools.partial(body, 0))
    pl.when(role_of() == 1)(functools.partial(body, 1))


def split_kernel(a_ref, b_ref, c_ref, d_ref, e_ref, keep_ref, send_ref):
    def total(at):
        return a_ref[at, :] + b_ref[at, :] + c_ref[at, :] + d_ref[at, :] + e_ref[at, :]

    low, high, tail = slice(0, ROWS), slice(ROWS, BLOCK), slice(BLOCK, BLOCK + LOSS)
    role = role_of()
    keep_ref[ROWS:, :] = total(tail)
    send_ref[ROWS:, :] = total(tail)

    @pl.when(role == 0)
    def _():
        keep_ref[:ROWS, :] = total(low)
        send_ref[:ROWS, :] = total(high)

    @pl.when(role == 1)
    def _():
        keep_ref[:ROWS, :] = total(high)
        send_ref[:ROWS, :] = total(low)


def post_kernel(q_ref, d_ref, keep_ref, come_ref, loss_ref, gq_ref, gd_ref):
    def project(out_ref, grad, values):
        unit, length = unit_rows(values)
        out_ref[...] = (grad - jnp.sum(grad * unit, axis=1, keepdims=True) * unit) / length

    def fill(gq, gd):
        project(gq_ref, gq[:ROWS, :], q_ref[...])
        project(gd_ref, gd[:ROWS, :], d_ref[...])
        loss_ref[...] = gd[ROWS : ROWS + 1, 0:1] * (1.0 / 16384)

    role = role_of()

    @pl.when(role == 0)
    def _():
        fill(keep_ref, come_ref)

    @pl.when(role == 1)
    def _():
        fill(come_ref, keep_ref)


def local(queries, documents, positives):
    piece = pltpu.VMEM((ROWS + PAD, WIDTH), BF16)
    keep, give = call(
        pre_kernel, "pre", [piece, piece], queries, documents, positives.reshape(1, ROWS)
    )
    come = swap(give)
    own = call(join_kernel, "join", pltpu.VMEM((BLOCK + PAD, WIDTH), BF16), near(keep), near(come))
    x = [own] + [None] * 7
    for bits in (4, 2, 1, 7):
        x[bits] = send(own, bits)
    y = [None] * 8
    for bits in (0, 4, 2, 1):
        y[bits] = swap(x[bits])
    x[6] = send(x[2], 4)
    x[3] = send(x[1], 2)
    x[5] = send(x[4], 1)
    for bits in (7, 6, 3, 5):
        y[bits] = swap(x[bits])
    x = [near(v) for v in x]
    y = [near(v) for v in y]

    e, stats = call(
        tile_kernel,
        "tile",
        [pltpu.VMEM((SIDE, SIDE), F32), pltpu.VMEM((CUBE, 2 * HALF, 128), F32)],
        *x,
        *y,
        scratch=[pltpu.VMEM((16, SIDE), F32)],
    )
    stats = lax.all_to_all(stats, "dp", 0, 0, axis_index_groups=SUM_GROUPS, tiled=True)

    def grads(chosen, name):
        return call(
            functools.partial(grad_kernel, chosen),
            name,
            [pltpu.VMEM((BLOCK + LOSS, WIDTH), F32)] * len(chosen),
            near(e),
            near(stats),
            *y,
            *[x[i] for i in chosen],
            scratch=[pltpu.VMEM((HALF, 128), F32)],
        )

    g6, g3, g5, g7 = grads((6, 3, 5, 7), "grad_far")
    r6, r3, r5, r7 = send(g6, 4), send(g3, 2), send(g5, 1), send(g7, 7)
    g4, g2, g1, g0 = grads((4, 2, 1, 0), "grad_near")
    r4 = send(g4 + r5, 4)
    r2 = send(g2 + r6, 2)
    r1 = send(g1 + r3, 1)
    part = pltpu.VMEM((ROWS + LOSS, WIDTH), F32)
    keep, give = call(
        split_kernel, "split", [part, part], *[near(v) for v in (g0, r4, r2, r1, r7)]
    )
    come = swap(give)
    loss, gq, gd = call(
        post_kernel,
        "post",
        [
            jax.ShapeDtypeStruct((1, 1), F32),
            jax.ShapeDtypeStruct((ROWS, WIDTH), F32),
            jax.ShapeDtypeStruct((ROWS, WIDTH), F32),
        ],
        queries,
        documents,
        near(keep),
        near(come),
    )
    return (loss.reshape(()), gq, gd)


def solution(mesh):
    placed = (P("dp", None), P("dp", None), P("dp"))
    return jax.shard_map(
        local,
        mesh=mesh,
        in_specs=placed,
        out_specs=(P(), P("dp", None), P("dp", None)),
        check_vma=False,
    )
```

time: 504 us -> 94.5 us (0.19)
  waiting for transfers between devices: 264 us -> 36.7 us
  matrix products: 113 us -> 0 us
  blocking collectives: 64.5 us -> 7.35 us
  starting transfers between devices: 0.08 us -> 30.2 us
  other arithmetic: 21.7 us -> 0.28 us
  local copies, waits for them, and re-layouts: 21.8 us -> 2.52 us
  Pallas kernels: 0 us -> 16.6 us
  between operations: 15.9 us -> 0.76 us
    reduce_scatter x1 -> x0, waiting for transfers between devices: 168 us -> none  [local(): lax.psum_scatter(20.0 * contract_rows(weights_of(rows, jnp.int32(0)), qb)...]
    dot_general x33 -> x0, matrix products: 113 us -> none  [the longest x16 52.7 us: add_grad(): jnp.dot(weights, rows, preferred_element_type=jnp.float32)]
    all_gather x1 -> x0, waiting for transfers between devices: 96 us -> none  [local(): alldocs = lax.all_gather(db, 'dp', axis=0, tiled=True)]
    psum x1 -> x0, blocking collectives: 64.5 us -> none  [local(): loss_sum = lax.psum(jnp.sum(lse - positive_score), 'dp')]
    ppermute x0 -> x24, waiting for transfers between devices: none -> 36.7 us  [the longest x14 32.4 us: send(): return lax.ppermute(value, 'dp', partners(bits))]
    ppermute x0 -> x24, starting transfers between devices: none -> 30.2 us  [the longest x14 24.8 us: send(): return lax.ppermute(value, 'dp', partners(bits))]
    pallas_call x0 -> x7, Pallas kernels: none -> 16.6 us  [call(): pl.pallas_call(kernel, name=name, out_shape=out_shape, scratch_shapes=scr...]
    gather x1 -> x0, local copies, waits for them, and re-layouts: 12.4 us -> none  [local(): picked = jnp.take(alldocs, positives, axis=0)]
  transfers between devices with their start and end apart: 2 -> 24, of which waited for: 2 -> 12; matrix products, arithmetic and copies ran while one was open for 15% -> 0% of each run, Pallas kernels for 0% -> 4%
where the time goes in v2:
time: 94.5 us; the launch traced here: 94.3 us
  waiting for transfers between devices  36.7 us (39%)
  starting transfers between devices  30.2 us (32%)
  Pallas kernels  16.6 us (18%)
  blocking collectives  7.35 us (8%)
  local copies, waits for them, and re-layouts  2.52 us (3%)
    ppermute x14, waiting for transfers between devices, send(): return lax.ppermute(value, 'dp', partners(bits))  32.4 us
    ppermute x14, starting transfers between devices, send(): return lax.ppermute(value, 'dp', partners(bits))  24.8 us
    pallas_call x7, Pallas kernels, call(): pl.pallas_call(kernel, name=name, out_shape=out_shape, scratch_shapes=scr...  16.6 us
    all_to_all x1, blocking collectives, local(): lax.all_to_all(stats, 'dp', 0, 0, axis_index_groups=SUM_GROUPS, tiled=True)  7.35 us
    ppermute x10, starting transfers between devices, swap(): return lax.ppermute(value, 'dp', SWAP)  5.38 us
    ppermute x10, waiting for transfers between devices, swap(): return lax.ppermute(value, 'dp', SWAP)  4.23 us
    unnamed x10, local copies, waits for them, and re-layouts  2.52 us
  transfers between devices with their start and end apart: 24, of which 12 were waited for; matrix products, arithmetic and copies ran while one was open for 0% of the time, Pallas kernels for 4%

profile of v2, /device:TPU:1, one launch (start us, length us, event | category | flops | bytes accessed | tf_op | source)
XLA Modules:
  0.0 94.3 jit_solution(1906678937473160704)
XLA Ops:
  0.6 0.9 copy-done
  1.6 0.9 copy-done.2
  2.5 0.7 copy-done.4
  3.3 1.5 %collective-permute-start = (bf16[144,768]{1,0:T(8,128)(2,1)S(1)}, bf16[144,768]{1,0:T(8,128)(2,1)S(1)}, u32[]{:S(2)}, u32[]{:S(2)}) collective-permute-start(bf16[144,768]{1,0:T(8,128)(2,1)S(1)} %get-tuple-element.21), channel_id=1, source_target_pairs={{0,1},{1,0},{2,3},{3,2},{4,5},{5,4},{6,7},{7,6},{8,9},{9,8},{10,11... | collective-permute-start | bytes 663560 | tf_op jit(solution)/shard_map/ppermute | solution.py:62
  4.8 1.1 %collective-permute-done.come_ref = bf16[144,768]{1,0:T(8,128)(2,1)S(1)} collective-permute-done((bf16[144,768]{1,0:T(8,128)(2,1)S(1)}, bf16[144,768]{1,0:T(8,128)(2,1)S(1)}, u32[]{:S(2)}, u32[]{:S(2)}) %collective-permute-start) | collective-permute-done | bytes 221216 | tf_op jit(solution)/shard_map/ppermute | solution.py:62
  6.0 8.6 %collective-permute-start.7 = (bf16[272,768]{1,0:T(8,128)(2,1)S(1)}, bf16[272,768]{1,0:T(8,128)(2,1)S(1)}, u32[]{:S(2)}, u32[]{:S(2)}) collective-permute-start(bf16[272,768]{1,0:T(8,128)(2,1)S(1)} %join.1.refs_0_.refs_13_), channel_id=1, source_target_pairs={{0,42},{1,127},{2,40},{3,125},{4,46},{5,123},{6,44},{7,121},{8,34}... | collective-permute-start | bytes 1253384 | tf_op jit(solution)/shard_map/ppermute | solution.py:58
  14.7 0.5 collective-permute-start.1
  15.2 4.9 %collective-permute-done.7.refs_7_.refs_13_ = bf16[272,768]{1,0:T(8,128)(2,1)S(1)} collective-permute-done((bf16[272,768]{1,0:T(8,128)(2,1)S(1)}, bf16[272,768]{1,0:T(8,128)(2,1)S(1)}, u32[]{:S(2)}, u32[]{:S(2)}) %collective-permute-start.7) | collective-permute-done | bytes 417824 | tf_op jit(solution)/shard_map/ppermute | solution.py:58
  20.1 4.6 %collective-permute-done.4.refs_4_.refs_10_ = bf16[272,768]{1,0:T(8,128)(2,1)S(1)} collective-permute-done((bf16[272,768]{1,0:T(8,128)(2,1)S(1)}, bf16[272,768]{1,0:T(8,128)(2,1)S(1)}, u32[]{:S(2)}, u32[]{:S(2)}) %collective-permute-start.4) | collective-permute-done | bytes 417824 | tf_op jit(solution)/shard_map/ppermute | solution.py:58
  24.7 2.6 %collective-permute-start.6 = (bf16[272,768]{1,0:T(8,128)(2,1)S(1)}, bf16[272,768]{1,0:T(8,128)(2,1)S(1)}, u32[]{:S(2)}, u32[]{:S(2)}) collective-permute-start(bf16[272,768]{1,0:T(8,128)(2,1)S(1)} %collective-permute-done.2.refs_2_.refs_11_), channel_id=1, source_target_pairs={{0,32},{1,97},{2,34},{3,99},{4,36},{5,101},{6,38},{7,103},{8,40},{... | collective-permute-start | bytes 1253384 | tf_op jit(solution)/shard_map/ppermute | solution.py:58
  27.3 1.9 %collective-permute-start.3 = (bf16[272,768]{1,0:T(8,128)(2,1)S(1)}, bf16[272,768]{1,0:T(8,128)(2,1)S(1)}, u32[]{:S(2)}, u32[]{:S(2)}) collective-permute-start(bf16[272,768]{1,0:T(8,128)(2,1)S(1)} %collective-permute-done.1.refs_1_.refs_12_), channel_id=1, source_target_pairs={{0,8},{1,25},{2,10},{3,27},{4,12},{5,29},{6,14},{7,31},{8,0},{9,17... | collective-permute-start | bytes 1253384 | tf_op jit(solution)/shard_map/ppermute | solution.py:58
  29.2 0.5 collective-permute-start.9
  29.7 3.1 %collective-permute-done.5.refs_5_.refs_12_ = bf16[272,768]{1,0:T(8,128)(2,1)S(1)} collective-permute-done((bf16[272,768]{1,0:T(8,128)(2,1)S(1)}, bf16[272,768]{1,0:T(8,128)(2,1)S(1)}, u32[]{:S(2)}, u32[]{:S(2)}) %collective-permute-start.5) | collective-permute-done | bytes 417824 | tf_op jit(solution)/shard_map/ppermute | solution.py:58
  33.4 1.9 %collective-permute-done.3.refs_3_.refs_11_ = bf16[272,768]{1,0:T(8,128)(2,1)S(1)} collective-permute-done((bf16[272,768]{1,0:T(8,128)(2,1)S(1)}, bf16[272,768]{1,0:T(8,128)(2,1)S(1)}, u32[]{:S(2)}, u32[]{:S(2)}) %collective-permute-start.3) | collective-permute-done | bytes 417824 | tf_op jit(solution)/shard_map/ppermute | solution.py:58
  35.4 1.7 %collective-permute-done.11.refs_11_.refs_5_ = bf16[272,768]{1,0:T(8,128)(2,1)S(1)} collective-permute-done((bf16[272,768]{1,0:T(8,128)(2,1)S(1)}, bf16[272,768]{1,0:T(8,128)(2,1)S(1)}, u32[]{:S(2)}, u32[]{:S(2)}) %collective-permute-start.11) | collective-permute-done | bytes 417824 | tf_op jit(solution)/shard_map/ppermute | solution.py:62
  37.1 7.2 %tile.1 = (f32[2048,2048]{1,0:T(8,128)S(1)}, f32[8,32,128]{2,1,0:T(8,128)S(1)}) custom-call(bf16[272,768]{1,0:T(8,128)(2,1)S(1)} %join.1.refs_0_.refs_13_, bf16[272,768]{1,0:T(8,128)(2,1)S(1)} %collective-permute-done.1.refs_1_.refs_12_, bf16[272,768]{1,0:T(8,128)(2,1)S(1)} %collective-permute-done.2.refs_2_.refs_11_, ...), custom_call_target="tpu_custom_call" | custom-call | tf_op jit(solution)/shard_map/tile/pallas_call | solution.py:70
  44.3 7.3 %all_to_all.5.refs_1_ = f32[8,32,128]{2,1,0:T(8,128)S(1)} all-to-all(f32[8,32,128]{2,1,0:T(8,128)S(1)} %get-tuple-element.23), channel_id=1, replica_groups={{0,2,8,10,32,34,40,42},{4,6,12,14,36,38,44,46},{16,18,24,26,48,50,56,58..., dimensions={0} | all-to-all | bytes 262144 | tf_op jit(solution)/shard_map/all_to_all | solution.py:302
  51.7 3.9 %grad_far.1 = (f32[264,768]{1,0:T(8,128)S(1)}, f32[264,768]{1,0:T(8,128)S(1)}, f32[264,768]{1,0:T(8,128)S(1)}, f32[264,768]{1,0:T(8,128)S(1)}) custom-call(f32[2048,2048]{1,0:T(8,128)S(1)} %get-tuple-element.22.refs_0_, f32[8,32,128]{2,1,0:T(8,128)S(1)} %all_to_all.5.refs_1_, bf16[272,768]{1,0:T(8,128)(2,1)S(1)} %collective-permute-done.8.refs_8_.refs_2_, ...), custom_call_target="tpu_custom_call" | custom-call | tf_op jit(solution)/shard_map/grad_far/pallas_call | solution.py:70
  55.6 1.7 %collective-permute-start.16 = (f32[264,768]{1,0:T(8,128)S(1)}, f32[264,768]{1,0:T(8,128)S(1)}, u32[]{:S(2)}, u32[]{:S(2)}) collective-permute-start(f32[264,768]{1,0:T(8,128)S(1)} %get-tuple-element.26), channel_id=1, source_target_pairs={{0,2},{1,7},{2,0},{3,5},{4,6},{5,3},{6,4},{7,1},{8,10},{9,15},{10,... | collective-permute-start | bytes 2433032 | tf_op jit(solution)/shard_map/ppermute | solution.py:58
  57.4 0.9 %collective-permute-start.18 = (f32[264,768]{1,0:T(8,128)S(1)}, f32[264,768]{1,0:T(8,128)S(1)}, u32[]{:S(2)}, u32[]{:S(2)}) collective-permute-start(f32[264,768]{1,0:T(8,128)S(1)} %get-tuple-element.28), channel_id=1, source_target_pairs={{0,32},{1,97},{2,34},{3,99},{4,36},{5,101},{6,38},{7,103},{8,40},{... | collective-permute-start | bytes 2433032 | tf_op jit(solution)/shard_map/ppermute | solution.py:58
  58.6 4.6 %collective-permute-start.22 = (f32[264,768]{1,0:T(8,128)S(1)}, f32[264,768]{1,0:T(8,128)S(1)}, u32[]{:S(2)}, u32[]{:S(2)}) collective-permute-start(f32[264,768]{1,0:T(8,128)S(1)} %get-tuple-element.31), channel_id=1, source_target_pairs={{0,42},{1,127},{2,40},{3,125},{4,46},{5,123},{6,44},{7,121},{8,34}... | collective-permute-start | bytes 2433032 | tf_op jit(solution)/shard_map/ppermute | solution.py:58
  63.2 3.7 %grad_near.1 = (f32[264,768]{1,0:T(8,128)S(1)}, f32[264,768]{1,0:T(8,128)S(1)}, f32[264,768]{1,0:T(8,128)S(1)}, f32[264,768]{1,0:T(8,128)S(1)}) custom-call(f32[2048,2048]{1,0:T(8,128)S(1)} %get-tuple-element.22.refs_0_, f32[8,32,128]{2,1,0:T(8,128)S(1)} %all_to_all.5.refs_1_, bf16[272,768]{1,0:T(8,128)(2,1)S(1)} %collective-permute-done.8.refs_8_.refs_2_, ...), custom_call_target="tpu_custom_call" | custom-call | tf_op jit(solution)/shard_map/grad_near/pallas_call | solution.py:70
  66.9 1.1 %collective-permute-done.16 = f32[264,768]{1,0:T(8,128)S(1)} collective-permute-done((f32[264,768]{1,0:T(8,128)S(1)}, f32[264,768]{1,0:T(8,128)S(1)}, u32[]{:S(2)}, u32[]{:S(2)}) %collective-permute-start.16) | collective-permute-done | bytes 811040 | tf_op jit(solution)/shard_map/ppermute | solution.py:58
  68.1 1.5 %collective-permute-start.17 = (f32[264,768]{1,0:T(8,128)S(1)}, f32[264,768]{1,0:T(8,128)S(1)}, u32[]{:S(2)}, u32[]{:S(2)}) collective-permute-start(f32[264,768]{1,0:T(8,128)S(1)} %add.9), channel_id=1, source_target_pairs={{0,32},{1,97},{2,34},{3,99},{4,36},{5,101},{6,38},{7,103},{8,40},{... | collective-permute-start | bytes 2433032 | tf_op jit(solution)/shard_map/ppermute | solution.py:58
  69.8 0.7 collective-permute-start.19
  71.0 1.3 %collective-permute-start.21 = (f32[264,768]{1,0:T(8,128)S(1)}, f32[264,768]{1,0:T(8,128)S(1)}, u32[]{:S(2)}, u32[]{:S(2)}) collective-permute-start(f32[264,768]{1,0:T(8,128)S(1)} %add.11), channel_id=1, source_target_pairs={{0,2},{1,7},{2,0},{3,5},{4,6},{5,3},{6,4},{7,1},{8,10},{9,15},{10,... | collective-permute-start | bytes 2433032 | tf_op jit(solution)/shard_map/ppermute | solution.py:58
  72.3 7.8 %collective-permute-done.22.e_ref = f32[264,768]{1,0:T(8,128)S(1)} collective-permute-done((f32[264,768]{1,0:T(8,128)S(1)}, f32[264,768]{1,0:T(8,128)S(1)}, u32[]{:S(2)}, u32[]{:S(2)}) %collective-permute-start.22) | collective-permute-done | bytes 811040 | tf_op jit(solution)/shard_map/ppermute | solution.py:58
  80.1 7.0 %collective-permute-done.17.b_ref = f32[264,768]{1,0:T(8,128)S(1)} collective-permute-done((f32[264,768]{1,0:T(8,128)S(1)}, f32[264,768]{1,0:T(8,128)S(1)}, u32[]{:S(2)}, u32[]{:S(2)}) %collective-permute-start.17) | collective-permute-done | bytes 811040 | tf_op jit(solution)/shard_map/ppermute | solution.py:58
  87.1 1.5 %collective-permute-done.19.c_ref = f32[264,768]{1,0:T(8,128)S(1)} collective-permute-done((f32[264,768]{1,0:T(8,128)S(1)}, f32[264,768]{1,0:T(8,128)S(1)}, u32[]{:S(2)}, u32[]{:S(2)}) %collective-permute-start.19) | collective-permute-done | bytes 811040 | tf_op jit(solution)/shard_map/ppermute | solution.py:58
  89.0 2.7 %collective-permute-start.23 = (f32[136,768]{1,0:T(8,128)S(1)}, f32[136,768]{1,0:T(8,128)S(1)}, u32[]{:S(2)}, u32[]{:S(2)}) collective-permute-start(f32[136,768]{1,0:T(8,128)S(1)} %get-tuple-element.33), channel_id=1, source_target_pairs={{0,1},{1,0},{2,3},{3,2},{4,5},{5,4},{6,7},{7,6},{8,9},{9,8},{10,11... | collective-permute-start | bytes 1253384 | tf_op jit(solution)/shard_map/ppermute | solution.py:62
  91.7 1.4 %collective-permute-done.23.come_ref = f32[136,768]{1,0:T(8,128)S(1)} collective-permute-done((f32[136,768]{1,0:T(8,128)S(1)}, f32[136,768]{1,0:T(8,128)S(1)}, u32[]{:S(2)}, u32[]{:S(2)}) %collective-permute-start.23) | collective-permute-done | bytes 417824 | tf_op jit(solution)/shard_map/ppermute | solution.py:62
  93.1 1.2 %post.1 = (f32[1,1]{1,0:T(1,128)}, f32[128,768]{1,0:T(8,128)}, f32[128,768]{1,0:T(8,128)}) custom-call(bf16[128,768]{1,0:T(8,128)(2,1)S(1)} %copy-done.1, bf16[128,768]{1,0:T(8,128)(2,1)S(1)} %copy-done.3, f32[136,768]{1,0:T(8,128)S(1)} %get-tuple-element.32.keep_ref, f32[136,768]{1,0:T(8,128)S(1)} %collective-permute-done.23.come_ref), custom_call_target="tpu_custom_call" | custom-call | tf_op jit(solution)/shard_map/post/pallas_call | solution.py:70
  (37 shorter events, 2.4 us)
Async XLA Ops:
  0.6 0.9 copy-start
  1.6 0.9 copy-start.2
  2.5 0.7 copy-start.4
  3.3 2.6 %collective-permute-start = (bf16[144,768]{1,0:T(8,128)(2,1)S(1)}, bf16[144,768]{1,0:T(8,128)(2,1)S(1)}, u32[]{:S(2)}, u32[]{:S(2)}) collective-permute-start(bf16[144,768]{1,0:T(8,128)(2,1)S(1)} %get-tuple-element.21), channel_id=1, source_target_pairs={{0,1},{1,0},{2,3},{3,2},{4,5},{5,4},{6,7},{7,6},{8,9},{9,8},{10,11... | collective-permute-start | bytes 663560 | tf_op jit(solution)/shard_map/ppermute | solution.py:62
  6.0 14.1 %collective-permute-start.7 = (bf16[272,768]{1,0:T(8,128)(2,1)S(1)}, bf16[272,768]{1,0:T(8,128)(2,1)S(1)}, u32[]{:S(2)}, u32[]{:S(2)}) collective-permute-start(bf16[272,768]{1,0:T(8,128)(2,1)S(1)} %join.1.refs_0_.refs_13_), channel_id=1, source_target_pairs={{0,42},{1,127},{2,40},{3,125},{4,46},{5,123},{6,44},{7,121},{8,34}... | collective-permute-start | bytes 1253384 | tf_op jit(solution)/shard_map/ppermute | solution.py:58
  14.5 10.1 %collective-permute-start.4 = (bf16[272,768]{1,0:T(8,128)(2,1)S(1)}, bf16[272,768]{1,0:T(8,128)(2,1)S(1)}, u32[]{:S(2)}, u32[]{:S(2)}) collective-permute-start(bf16[272,768]{1,0:T(8,128)(2,1)S(1)} %join.1.refs_0_.refs_13_), channel_id=1, source_target_pairs={{0,32},{1,97},{2,34},{3,99},{4,36},{5,101},{6,38},{7,103},{8,40},{... | collective-permute-start | bytes 1253384 | tf_op jit(solution)/shard_map/ppermute | solution.py:58
  14.7 9.9 %collective-permute-start.8 = (bf16[272,768]{1,0:T(8,128)(2,1)S(1)}, bf16[272,768]{1,0:T(8,128)(2,1)S(1)}, u32[]{:S(2)}, u32[]{:S(2)}) collective-permute-start(bf16[272,768]{1,0:T(8,128)(2,1)S(1)} %join.1.refs_0_.refs_13_), channel_id=1, source_target_pairs={{0,1},{1,0},{2,3},{3,2},{4,5},{5,4},{6,7},{7,6},{8,9},{9,8},{10,11... | collective-permute-start | bytes 1253384 | tf_op jit(solution)/shard_map/ppermute | solution.py:62
  14.7 10.0 %collective-permute-start.2 = (bf16[272,768]{1,0:T(8,128)(2,1)S(1)}, bf16[272,768]{1,0:T(8,128)(2,1)S(1)}, u32[]{:S(2)}, u32[]{:S(2)}) collective-permute-start(bf16[272,768]{1,0:T(8,128)(2,1)S(1)} %join.1.refs_0_.refs_13_), channel_id=1, source_target_pairs={{0,8},{1,25},{2,10},{3,27},{4,12},{5,29},{6,14},{7,31},{8,0},{9,17... | collective-permute-start | bytes 1253384 | tf_op jit(solution)/shard_map/ppermute | solution.py:58
  14.7 12.5 %collective-permute-start.1 = (bf16[272,768]{1,0:T(8,128)(2,1)S(1)}, bf16[272,768]{1,0:T(8,128)(2,1)S(1)}, u32[]{:S(2)}, u32[]{:S(2)}) collective-permute-start(bf16[272,768]{1,0:T(8,128)(2,1)S(1)} %join.1.refs_0_.refs_13_), channel_id=1, source_target_pairs={{0,2},{1,7},{2,0},{3,5},{4,6},{5,3},{6,4},{7,1},{8,10},{9,15},{10,... | collective-permute-start | bytes 1253384 | tf_op jit(solution)/shard_map/ppermute | solution.py:58
  20.1 9.1 %collective-permute-start.15 = (bf16[272,768]{1,0:T(8,128)(2,1)S(1)}, bf16[272,768]{1,0:T(8,128)(2,1)S(1)}, u32[]{:S(2)}, u32[]{:S(2)}) collective-permute-start(bf16[272,768]{1,0:T(8,128)(2,1)S(1)} %collective-permute-done.7.refs_7_.refs_13_), channel_id=1, source_target_pairs={{0,1},{1,0},{2,3},{3,2},{4,5},{5,4},{6,7},{7,6},{8,9},{9,8},{10,11... | collective-permute-start | bytes 1253384 | tf_op jit(solution)/shard_map/ppermute | solution.py:62
  24.7 4.5 %collective-permute-start.12 = (bf16[272,768]{1,0:T(8,128)(2,1)S(1)}, bf16[272,768]{1,0:T(8,128)(2,1)S(1)}, u32[]{:S(2)}, u32[]{:S(2)}) collective-permute-start(bf16[272,768]{1,0:T(8,128)(2,1)S(1)} %collective-permute-done.4.refs_4_.refs_10_), channel_id=1, source_target_pairs={{0,1},{1,0},{2,3},{3,2},{4,5},{5,4},{6,7},{7,6},{8,9},{9,8},{10,11... | collective-permute-start | bytes 1253384 | tf_op jit(solution)/shard_map/ppermute | solution.py:62
  24.7 8.1 %collective-permute-start.5 = (bf16[272,768]{1,0:T(8,128)(2,1)S(1)}, bf16[272,768]{1,0:T(8,128)(2,1)S(1)}, u32[]{:S(2)}, u32[]{:S(2)}) collective-permute-start(bf16[272,768]{1,0:T(8,128)(2,1)S(1)} %collective-permute-done.4.refs_4_.refs_10_), channel_id=1, source_target_pairs={{0,2},{1,7},{2,0},{3,5},{4,6},{5,3},{6,4},{7,1},{8,10},{9,15},{10,... | collective-permute-start | bytes 1253384 | tf_op jit(solution)/shard_map/ppermute | solution.py:58
  24.7 8.5 %collective-permute-start.6 = (bf16[272,768]{1,0:T(8,128)(2,1)S(1)}, bf16[272,768]{1,0:T(8,128)(2,1)S(1)}, u32[]{:S(2)}, u32[]{:S(2)}) collective-permute-start(bf16[272,768]{1,0:T(8,128)(2,1)S(1)} %collective-permute-done.2.refs_2_.refs_11_), channel_id=1, source_target_pairs={{0,32},{1,97},{2,34},{3,99},{4,36},{5,101},{6,38},{7,103},{8,40},{... | collective-permute-start | bytes 1253384 | tf_op jit(solution)/shard_map/ppermute | solution.py:58
  27.3 8.1 %collective-permute-start.3 = (bf16[272,768]{1,0:T(8,128)(2,1)S(1)}, bf16[272,768]{1,0:T(8,128)(2,1)S(1)}, u32[]{:S(2)}, u32[]{:S(2)}) collective-permute-start(bf16[272,768]{1,0:T(8,128)(2,1)S(1)} %collective-permute-done.1.refs_1_.refs_12_), channel_id=1, source_target_pairs={{0,8},{1,25},{2,10},{3,27},{4,12},{5,29},{6,14},{7,31},{8,0},{9,17... | collective-permute-start | bytes 1253384 | tf_op jit(solution)/shard_map/ppermute | solution.py:58
  29.2 6.2 %collective-permute-start.10 = (bf16[272,768]{1,0:T(8,128)(2,1)S(1)}, bf16[272,768]{1,0:T(8,128)(2,1)S(1)}, u32[]{:S(2)}, u32[]{:S(2)}) collective-permute-start(bf16[272,768]{1,0:T(8,128)(2,1)S(1)} %collective-permute-done.2.refs_2_.refs_11_), channel_id=1, source_target_pairs={{0,1},{1,0},{2,3},{3,2},{4,5},{5,4},{6,7},{7,6},{8,9},{9,8},{10,11... | collective-permute-start | bytes 1253384 | tf_op jit(solution)/shard_map/ppermute | solution.py:62
  29.2 6.2 %collective-permute-start.9 = (bf16[272,768]{1,0:T(8,128)(2,1)S(1)}, bf16[272,768]{1,0:T(8,128)(2,1)S(1)}, u32[]{:S(2)}, u32[]{:S(2)}) collective-permute-start(bf16[272,768]{1,0:T(8,128)(2,1)S(1)} %collective-permute-done.1.refs_1_.refs_12_), channel_id=1, source_target_pairs={{0,1},{1,0},{2,3},{3,2},{4,5},{5,4},{6,7},{7,6},{8,9},{9,8},{10,11... | collective-permute-start | bytes 1253384 | tf_op jit(solution)/shard_map/ppermute | solution.py:62
  32.8 2.6 %collective-permute-start.13 = (bf16[272,768]{1,0:T(8,128)(2,1)S(1)}, bf16[272,768]{1,0:T(8,128)(2,1)S(1)}, u32[]{:S(2)}, u32[]{:S(2)}) collective-permute-start(bf16[272,768]{1,0:T(8,128)(2,1)S(1)} %collective-permute-done.5.refs_5_.refs_12_), channel_id=1, source_target_pairs={{0,1},{1,0},{2,3},{3,2},{4,5},{5,4},{6,7},{7,6},{8,9},{9,8},{10,11... | collective-permute-start | bytes 1253384 | tf_op jit(solution)/shard_map/ppermute | solution.py:62
  33.2 2.2 %collective-permute-start.14 = (bf16[272,768]{1,0:T(8,128)(2,1)S(1)}, bf16[272,768]{1,0:T(8,128)(2,1)S(1)}, u32[]{:S(2)}, u32[]{:S(2)}) collective-permute-start(bf16[272,768]{1,0:T(8,128)(2,1)S(1)} %collective-permute-done.6.refs_6_.refs_10_), channel_id=1, source_target_pairs={{0,1},{1,0},{2,3},{3,2},{4,5},{5,4},{6,7},{7,6},{8,9},{9,8},{10,11... | collective-permute-start | bytes 1253384 | tf_op jit(solution)/shard_map/ppermute | solution.py:62
  35.4 1.8 %collective-permute-start.11 = (bf16[272,768]{1,0:T(8,128)(2,1)S(1)}, bf16[272,768]{1,0:T(8,128)(2,1)S(1)}, u32[]{:S(2)}, u32[]{:S(2)}) collective-permute-start(bf16[272,768]{1,0:T(8,128)(2,1)S(1)} %collective-permute-done.3.refs_3_.refs_11_), channel_id=1, source_target_pairs={{0,1},{1,0},{2,3},{3,2},{4,5},{5,4},{6,7},{7,6},{8,9},{9,8},{10,11... | collective-permute-start | bytes 1253384 | tf_op jit(solution)/shard_map/ppermute | solution.py:62
  55.6 37.5 %copy-start.1 = (bf16[128,768]{1,0:T(8,128)(2,1)S(1)}, bf16[128,768]{1,0:T(8,128)(2,1)}, u32[]{:S(2)}) copy-start(bf16[128,768]{1,0:T(8,128)(2,1)} %q_ref.3) | copy-start | bytes 589828
  55.6 37.4 %copy-start.3 = (bf16[128,768]{1,0:T(8,128)(2,1)S(1)}, bf16[128,768]{1,0:T(8,128)(2,1)}, u32[]{:S(2)}) copy-start(bf16[128,768]{1,0:T(8,128)(2,1)} %d_ref.3) | copy-start | bytes 589828
  55.6 12.4 %collective-permute-start.16 = (f32[264,768]{1,0:T(8,128)S(1)}, f32[264,768]{1,0:T(8,128)S(1)}, u32[]{:S(2)}, u32[]{:S(2)}) collective-permute-start(f32[264,768]{1,0:T(8,128)S(1)} %get-tuple-element.26), channel_id=1, source_target_pairs={{0,2},{1,7},{2,0},{3,5},{4,6},{5,3},{6,4},{7,1},{8,10},{9,15},{10,... | collective-permute-start | bytes 2433032 | tf_op jit(solution)/shard_map/ppermute | solution.py:58
  57.4 12.3 %collective-permute-start.18 = (f32[264,768]{1,0:T(8,128)S(1)}, f32[264,768]{1,0:T(8,128)S(1)}, u32[]{:S(2)}, u32[]{:S(2)}) collective-permute-start(f32[264,768]{1,0:T(8,128)S(1)} %get-tuple-element.28), channel_id=1, source_target_pairs={{0,32},{1,97},{2,34},{3,99},{4,36},{5,101},{6,38},{7,103},{8,40},{... | collective-permute-start | bytes 2433032 | tf_op jit(solution)/shard_map/ppermute | solution.py:58
  58.3 12.6 %collective-permute-start.20 = (f32[264,768]{1,0:T(8,128)S(1)}, f32[264,768]{1,0:T(8,128)S(1)}, u32[]{:S(2)}, u32[]{:S(2)}) collective-permute-start(f32[264,768]{1,0:T(8,128)S(1)} %get-tuple-element.30), channel_id=1, source_target_pairs={{0,8},{1,25},{2,10},{3,27},{4,12},{5,29},{6,14},{7,31},{8,0},{9,17... | collective-permute-start | bytes 2433032 | tf_op jit(solution)/shard_map/ppermute | solution.py:58
  58.6 21.5 %collective-permute-start.22 = (f32[264,768]{1,0:T(8,128)S(1)}, f32[264,768]{1,0:T(8,128)S(1)}, u32[]{:S(2)}, u32[]{:S(2)}) collective-permute-start(f32[264,768]{1,0:T(8,128)S(1)} %get-tuple-element.31), channel_id=1, source_target_pairs={{0,42},{1,127},{2,40},{3,125},{4,46},{5,123},{6,44},{7,121},{8,34}... | collective-permute-start | bytes 2433032 | tf_op jit(solution)/shard_map/ppermute | solution.py:58
  68.1 19.0 %collective-permute-start.17 = (f32[264,768]{1,0:T(8,128)S(1)}, f32[264,768]{1,0:T(8,128)S(1)}, u32[]{:S(2)}, u32[]{:S(2)}) collective-permute-start(f32[264,768]{1,0:T(8,128)S(1)} %add.9), channel_id=1, source_target_pairs={{0,32},{1,97},{2,34},{3,99},{4,36},{5,101},{6,38},{7,103},{8,40},{... | collective-permute-start | bytes 2433032 | tf_op jit(solution)/shard_map/ppermute | solution.py:58
  69.8 18.9 %collective-permute-start.19 = (f32[264,768]{1,0:T(8,128)S(1)}, f32[264,768]{1,0:T(8,128)S(1)}, u32[]{:S(2)}, u32[]{:S(2)}) collective-permute-start(f32[264,768]{1,0:T(8,128)S(1)} %add.10), channel_id=1, source_target_pairs={{0,8},{1,25},{2,10},{3,27},{4,12},{5,29},{6,14},{7,31},{8,0},{9,17... | collective-permute-start | bytes 2433032 | tf_op jit(solution)/shard_map/ppermute | solution.py:58
  71.0 17.6 %collective-permute-start.21 = (f32[264,768]{1,0:T(8,128)S(1)}, f32[264,768]{1,0:T(8,128)S(1)}, u32[]{:S(2)}, u32[]{:S(2)}) collective-permute-start(f32[264,768]{1,0:T(8,128)S(1)} %add.11), channel_id=1, source_target_pairs={{0,2},{1,7},{2,0},{3,5},{4,6},{5,3},{6,4},{7,1},{8,10},{9,15},{10,... | collective-permute-start | bytes 2433032 | tf_op jit(solution)/shard_map/ppermute | solution.py:58
  89.0 4.1 %collective-permute-start.23 = (f32[136,768]{1,0:T(8,128)S(1)}, f32[136,768]{1,0:T(8,128)S(1)}, u32[]{:S(2)}, u32[]{:S(2)}) collective-permute-start(f32[136,768]{1,0:T(8,128)S(1)} %get-tuple-element.33), channel_id=1, source_target_pairs={{0,1},{1,0},{2,3},{3,2},{4,5},{5,4},{6,7},{7,6},{8,9},{9,8},{10,11... | collective-permute-start | bytes 1253384 | tf_op jit(solution)/shard_map/ppermute | solution.py:62
